TPU v7x, 32 devices: a whole 2x2x4 slice. The times are simulated.
32 devices in a mesh: ep: 8 (over y, x, core), tp: 4 (over z).
Axes of the slice: x: 2, y: 2, z: 4, core: 2. Of those that a mesh axis runs over, the one named last changes fastest.
Arguments:
- query: bfloat16 [3, 256, 8192], P(None, 'ep', 'tp'), may hold values from -110 to 110
- step_key_value: bfloat16 [3, 2, 256, 512], P(None, None, 'ep', 'tp'), may hold values from -5 to 5
- key_value_cache: bfloat16 [2, 256, 128, 512], P(None, 'ep', None, 'tp'), may hold values from -5 to 5
- lengths: int32 [256], P('ep'), may hold values from 2 to 128, as said below
- hidden_in: bfloat16 [3, 256, 4096], P(None, ('ep', 'tp')), may hold values from -3 to 3
- norm_gain: float32 [4096], replicated, may hold values from 0.5 to 1.5
- w_out: bfloat16 [8192, 4096], P('tp', 'ep'), may hold values from -0.1875 to 0.1875
- routes: int32 [3, 256, 8], P(None, ('ep', 'tp')), may hold values from 0 to 31, all different within a row; in each aligned block of 8 rows (0 to 7, 8 to 15, ..., all dimensions but the last counted through in order) at most 8 rows name the same one
- gate_scores: float32 [3, 256, 8], P(None, ('ep', 'tp')), may hold values from 0.1 to 1
- expert_gate: bfloat16 [32, 4096, 768], P(('ep', 'tp')), may hold values from -0.09375 to 0.09375
- expert_up: bfloat16 [32, 4096, 768], P(('ep', 'tp')), may hold values from -0.09375 to 0.09375
- expert_down: bfloat16 [32, 768, 4096], P(('ep', 'tp')), may hold values from -0.21875 to 0.21875
Outputs:
- layer_out: bfloat16 [3, 256, 4096], P(None, ('ep', 'tp'))
Inputs may be any that keep to these rules, and one draw needn't show every extreme that they name: `lengths`: every row has at least two filled cache positions, and some row fills all 128. `routes`: A row names 8 different experts. Within one step, the 8 rows of one device (aligned blocks of rows) name any one expert at most 8 times.
All inputs are finite; a program needn't handle non-finite values.
Results may differ from a plain program's by a relative error of at most 0.007.
Values may be sent and summed in bfloat16 or wider, within the bound.
A program may use at most 128 MiB of HBM per device.

v0:
```python
import jax
import jax.numpy as jnp
from jax import lax
from jax.sharding import PartitionSpec as P

HEAD_SIZE = 128
TOPK = 8
SLOTS = 256
DECODE_STEPS = 3


masked_score = -1e30
norm_eps = 1e-06


def per_device(
    query,
    step_key_value,
    key_value_cache,
    lengths,
    hidden_in,
    norm_gain,
    w_out,
    routes,
    gate_scores,
    expert_gate,
    expert_up,
    expert_down,
):
    ep_count = lax.axis_size("ep")
    tp_count = lax.axis_size("tp")
    row_dev = query.shape[1]
    row_own = hidden_in.shape[1]
    width = hidden_in.shape[2]
    heads_dev = query.shape[2] // HEAD_SIZE
    cache_len = key_value_cache.shape[2]
    expert_count = ep_count * tp_count * expert_gate.shape[0]
    capacity = SLOTS // expert_count
    score_scale = HEAD_SIZE ** (-0.5)
    stored_keys = key_value_cache[0]
    stored_values = key_value_cache[1]
    usable = jnp.arange(cache_len, dtype=jnp.int32)[None, :] < lengths[:, None]
    gate_weights = expert_gate[0]
    up_weights = expert_up[0]
    down_weights = expert_down[0]
    results = []
    for decode_step in range(DECODE_STEPS):
        query_rows = query[decode_step].reshape(row_dev, heads_dev, HEAD_SIZE)
        incoming_keys = step_key_value[: decode_step + 1, 0]
        incoming_values = step_key_value[: decode_step + 1, 1]
        cache_scores = (
            jnp.einsum("rhd,rjd->rhj", query_rows, stored_keys, preferred_element_type=jnp.float32)
            * score_scale
        )
        cache_scores = jnp.where(usable[:, None, :], cache_scores, masked_score)
        fresh_scores = (
            jnp.einsum(
                "rhd,jrd->rhj", query_rows, incoming_keys, preferred_element_type=jnp.float32
            )
            * score_scale
        )
        scores = jnp.concatenate([cache_scores, fresh_scores], axis=-1)
        top = jnp.max(scores, axis=-1, keepdims=True)
        raised = jnp.exp(scores - top)
        probs = (raised / jnp.sum(raised, axis=-1, keepdims=True)).astype(jnp.bfloat16)
        attended = jnp.einsum(
            "rhj,rjd->rhd",
            probs[..., :cache_len],
            stored_values,
            preferred_element_type=jnp.float32,
        )
        attended = attended + jnp.einsum(
            "rhj,jrd->rhd",
            probs[..., cache_len:],
            incoming_values,
            preferred_element_type=jnp.float32,
        )
        attended = attended.astype(jnp.bfloat16).reshape(row_dev, heads_dev * HEAD_SIZE)
        partial_sums = jnp.dot(
            lax.all_gather(attended, "ep", axis=0, tiled=True),
            w_out,
            preferred_element_type=jnp.float32,
        )
        grouped = partial_sums.reshape(ep_count, tp_count, row_own, -1)
        summed = lax.psum_scatter(grouped, "tp", scatter_dimension=1, tiled=True)
        projected = summed.reshape(ep_count, row_own, -1).astype(jnp.bfloat16)
        row_major = lax.all_to_all(
            projected, "ep", split_axis=0, concat_axis=2, tiled=True
        ).reshape(row_own, width)
        residual = hidden_in[decode_step].astype(jnp.float32) + row_major.astype(jnp.float32)
        mean_square = jnp.mean(residual * residual, axis=-1, keepdims=True)
        normed = (residual * lax.rsqrt(mean_square + norm_eps) * norm_gain).astype(jnp.bfloat16)
        weights = gate_scores[decode_step] / jnp.sum(
            gate_scores[decode_step], axis=-1, keepdims=True
        )
        expert_ids = routes[decode_step].reshape(-1)
        assigned = expert_ids.shape[0]
        matches = (
            expert_ids[:, None] == jnp.arange(expert_count, dtype=jnp.int32)[None, :]
        ).astype(jnp.int32)
        earlier = jnp.cumsum(matches, axis=0) - matches
        slot_rank = jnp.sum(earlier * matches, axis=1)
        slot_index = expert_ids * capacity + slot_rank
        slot_onehot = (
            slot_index[:, None] == jnp.arange(expert_count * capacity, dtype=jnp.int32)[None, :]
        ).astype(jnp.bfloat16)
        row_onehot = (
            (jnp.arange(assigned, dtype=jnp.int32) // TOPK)[:, None]
            == jnp.arange(row_own, dtype=jnp.int32)[None, :]
        ).astype(jnp.bfloat16)
        selector = jnp.einsum(
            "as,ar->sr", slot_onehot, row_onehot, preferred_element_type=jnp.float32
        ).astype(jnp.bfloat16)
        outgoing = jnp.dot(selector, normed, preferred_element_type=jnp.float32).astype(
            jnp.bfloat16
        )
        outgoing = outgoing.reshape(expert_count, capacity, width)
        arrived = lax.all_to_all(outgoing, ("ep", "tp"), split_axis=0, concat_axis=0, tiled=True)
        flat_rows = arrived.reshape(-1, width)
        gate_act = jnp.dot(flat_rows, gate_weights, preferred_element_type=jnp.float32)
        up_act = jnp.dot(flat_rows, up_weights, preferred_element_type=jnp.float32)
        hidden = (jax.nn.silu(gate_act) * up_act).astype(jnp.bfloat16)
        expert_out = jnp.dot(hidden, down_weights, preferred_element_type=jnp.float32).astype(
            jnp.bfloat16
        )
        returned = lax.all_to_all(
            expert_out.reshape(arrived.shape), ("ep", "tp"), split_axis=0, concat_axis=0, tiled=True
        )
        returned = returned.reshape(expert_count * capacity, width)
        selected = returned[slot_index].astype(jnp.float32) * weights.reshape(-1)[:, None]
        expert_mix = jnp.sum(selected.reshape(row_own, TOPK, width), axis=1)
        results.append((residual + expert_mix).astype(jnp.bfloat16))
    return jnp.stack(results)


def solution(mesh):
    placed = (
        P(None, "ep", "tp"),
        P(None, None, "ep", "tp"),
        P(None, "ep", None, "tp"),
        P("ep"),
        P(None, ("ep", "tp"), None),
        P(),
        P("tp", "ep"),
        P(None, ("ep", "tp"), None),
        P(None, ("ep", "tp"), None),
        P(("ep", "tp"), None, None),
        P(("ep", "tp"), None, None),
        P(("ep", "tp"), None, None),
    )
    return jax.shard_map(
        per_device,
        mesh=mesh,
        in_specs=placed,
        out_specs=P(None, ("ep", "tp"), None),
        check_vma=False,
    )
```

profile of v0, /device:TPU:0, one launch (start us, length us, event | category | flops | bytes accessed | tf_op | source)
XLA Modules:
  0.0 522.8 jit_solution(6278667925909246458)
XLA Ops:
  17.8 4.4 fusion.169
  49.2 7.8 %all-gather.4.cloned.1.call-done = bf16[256,2048]{1,0:T(8,128)(2,1)} async-done(((bf16[32,2048]{1,0:T(8,128)(2,1)}), bf16[256,2048]{1,0:T(8,128)(2,1)}) %all-gather.4.cloned.1.call-update) | async-done | bytes 1048592 | tf_op jit(solution)/shard_map/all_gather | solution.py:80
  58.9 23.5 %all-gather.6.cloned.1.call-done = bf16[256,2048]{1,0:T(8,128)(2,1)} async-done(((bf16[32,2048]{1,0:T(8,128)(2,1)}), bf16[256,2048]{1,0:T(8,128)(2,1)}) %all-gather.6.cloned.1.call-update) | async-done | bytes 1048592 | tf_op jit(solution)/shard_map/all_gather | solution.py:80
  84.3 23.5 %all-gather.8.cloned.1.call-done = bf16[256,2048]{1,0:T(8,128)(2,1)} async-done(((bf16[32,2048]{1,0:T(8,128)(2,1)}), bf16[256,2048]{1,0:T(8,128)(2,1)}) %all-gather.8.cloned.1.call-update) | async-done | bytes 1048592 | tf_op jit(solution)/shard_map/all_gather | solution.py:80
  110.5 61.5 %all-reduce.5 = (bf16[8,4,8,512]{3,2,1,0:T(8,128)(2,1)S(1)}, bf16[8,4,8,512]{3,2,1,0:T(8,128)(2,1)S(1)}, bf16[8,4,8,512]{3,2,1,0:T(8,128)(2,1)S(1)}) all-reduce(f32[8,4,8,512]{3,2,1,0:T(8,128)} %bitcast.299, f32[8,4,8,512]{3,2,1,0:T(8,128)S(1)} %bitcast.297, ...), channel_id=4, replica_groups=mesh['ep'=8,'tp'=4] {'tp'}, use_global_device_ids=true, to_apply=%region_20.21.clone | all-reduce | flops 393216 | bytes 2359296
  184.9 4.9 all-to-all-done.3
  193.2 4.9 all-to-all-done.6
  206.6 44.5 %all-to-all-done.4 = bf16[32,8,4096]{2,1,0:T(8,128)(2,1)S(1)} async-done(((bf16[32,8,4096]{2,1,0:T(8,128)(2,1)}), bf16[32,8,4096]{2,1,0:T(8,128)(2,1)S(1)}, u32[]{:S(2)}, u32[]{:S(2)}) %all-to-all-start.4) | async-done | bytes 2097184 | tf_op jit(solution)/shard_map/all_to_all | solution.py:118
  251.0 4.3 all-to-all-start.7
  258.2 44.5 %all-to-all-done.7 = bf16[32,8,4096]{2,1,0:T(8,128)(2,1)} async-done(((bf16[32,8,4096]{2,1,0:T(8,128)(2,1)}), bf16[32,8,4096]{2,1,0:T(8,128)(2,1)}, u32[]{:S(2)}, u32[]{:S(2)}) %all-to-all-start.7) | async-done | bytes 2097184 | tf_op jit(solution)/shard_map/all_to_all | solution.py:118
  302.7 4.4 all-to-all-start.1
  307.1 5.5 %fusion.14 = f32[256,768]{1,0:T(8,128)} fusion(bf16[1,4096,768]{2,1,0:T(8,128)(2,1)} %param.21, bf16[32,8,4096]{2,1,0:T(8,128)(2,1)S(1)} %all-to-all-done.4), kind=kOutput, calls=%fused_computation.17 | convolution fusion | flops 1610612736 | bytes 9175040 | tf_op jit(solution)/shard_map/dot_general | solution.py:120
  312.6 10.7 %fusion.30 = bf16[32,8,4096]{2,1,0:T(8,128)(2,1)} fusion(bf16[1,768,4096]{2,1,0:T(8,128)(2,1)} %param.23, bf16[1,4096,768]{2,1,0:T(8,128)(2,1)} %param.22, bf16[32,8,4096]{2,1,0:T(8,128)(2,1)S(1)} %all-to-all-done.4, f32[256,768]{1,0:T(8,128)} %fusion.14), kind=kOutput, calls=%fused_computation.28 | convolution fusion | flops 3223453696 | bytes 17563648 | tf_op jit(solution)/shard_map/dot_general | solution.py:123
  323.3 31.1 %all-to-all-done.1 = bf16[32,8,4096]{2,1,0:T(8,128)(2,1)} async-done(((bf16[32,8,4096]{2,1,0:T(8,128)(2,1)}), bf16[32,8,4096]{2,1,0:T(8,128)(2,1)}, u32[]{:S(2)}, u32[]{:S(2)}) %all-to-all-start.1) | async-done | bytes 2097184 | tf_op jit(solution)/shard_map/all_to_all | solution.py:118
  354.4 4.3 all-to-all-start.5
  358.8 6.1 %fusion.12 = f32[256,768]{1,0:T(8,128)} fusion(bf16[1,4096,768]{2,1,0:T(8,128)(2,1)} %param.21, bf16[32,8,4096]{2,1,0:T(8,128)(2,1)} %all-to-all-done.7), kind=kOutput, calls=%fused_computation.15 | convolution fusion | flops 1610612736 | bytes 9175040 | tf_op jit(solution)/shard_map/dot_general | solution.py:120
  364.9 11.3 %fusion.27 = bf16[32,8,4096]{2,1,0:T(8,128)(2,1)} fusion(bf16[1,768,4096]{2,1,0:T(8,128)(2,1)} %param.23, bf16[1,4096,768]{2,1,0:T(8,128)(2,1)} %param.22, bf16[32,8,4096]{2,1,0:T(8,128)(2,1)} %all-to-all-done.7, f32[256,768]{1,0:T(8,128)} %fusion.12), kind=kOutput, calls=%fused_computation.27 | convolution fusion | flops 3223453696 | bytes 17563648 | tf_op jit(solution)/shard_map/dot_general | solution.py:123
  376.2 30.1 %all-to-all-done.5 = bf16[32,8,4096]{2,1,0:T(8,128)(2,1)S(1)} async-done(((bf16[32,8,4096]{2,1,0:T(8,128)(2,1)}), bf16[32,8,4096]{2,1,0:T(8,128)(2,1)S(1)}, u32[]{:S(2)}, u32[]{:S(2)}) %all-to-all-start.5) | async-done | bytes 2097184 | tf_op jit(solution)/shard_map/all_to_all | solution.py:126
  406.3 4.3 all-to-all-start.8
  410.6 6.1 %fusion.16 = f32[256,768]{1,0:T(8,128)} fusion(bf16[1,4096,768]{2,1,0:T(8,128)(2,1)} %param.21, bf16[32,8,4096]{2,1,0:T(8,128)(2,1)} %all-to-all-done.1), kind=kOutput, calls=%fused_computation.19 | convolution fusion | flops 1610612736 | bytes 9175040 | tf_op jit(solution)/shard_map/dot_general | solution.py:120
  416.7 11.3 %fusion.33 = bf16[32,8,4096]{2,1,0:T(8,128)(2,1)} fusion(bf16[1,768,4096]{2,1,0:T(8,128)(2,1)} %param.23, bf16[1,4096,768]{2,1,0:T(8,128)(2,1)} %param.22, bf16[32,8,4096]{2,1,0:T(8,128)(2,1)} %all-to-all-done.1, f32[256,768]{1,0:T(8,128)} %fusion.16), kind=kOutput, calls=%fused_computation.29 | convolution fusion | flops 3223453696 | bytes 17563648 | tf_op jit(solution)/shard_map/dot_general | solution.py:123
  428.0 29.5 %all-to-all-done.8 = bf16[32,8,4096]{2,1,0:T(8,128)(2,1)} async-done(((bf16[32,8,4096]{2,1,0:T(8,128)(2,1)}), bf16[32,8,4096]{2,1,0:T(8,128)(2,1)}, u32[]{:S(2)}, u32[]{:S(2)}) %all-to-all-start.8) | async-done | bytes 2097184 | tf_op jit(solution)/shard_map/all_to_all | solution.py:126
  457.5 4.8 all-to-all-start.2
  467.8 41.8 %all-to-all-done.2 = bf16[32,8,4096]{2,1,0:T(8,128)(2,1)} async-done(((bf16[32,8,4096]{2,1,0:T(8,128)(2,1)}), bf16[32,8,4096]{2,1,0:T(8,128)(2,1)}, u32[]{:S(2)}, u32[]{:S(2)}) %all-to-all-start.2) | async-done | bytes 2097184 | tf_op jit(solution)/shard_map/all_to_all | solution.py:126
  (166 shorter events, 84.0 us)
Async XLA Ops:
  6.5 50.4 %copy-start = (bf16[2048,512]{1,0:T(8,128)(2,1)S(1)}, bf16[2048,512]{1,0:T(8,128)(2,1)}, u32[]{:S(2)}) copy-start(bf16[2048,512]{1,0:T(8,128)(2,1)} %param.18) | copy-start | bytes 6291460
  6.5 50.4 %all-gather.4.cloned.1.call-start = ((), (), s32[]{:S(2)}) async-start(), calls=%async_computation.9 | async-start | bytes 1179648 | tf_op jit(solution)/shard_map/all_gather | solution.py:80
  30.6 51.8 %all-gather.6.cloned.1.call-start = ((), (), s32[]{:S(2)}) async-start(), calls=%async_computation.10 | async-start | bytes 1179648 | tf_op jit(solution)/shard_map/all_gather | solution.py:80
  39.5 68.3 %all-gather.8.cloned.1.call-start = ((), (), s32[]{:S(2)}) async-start(), calls=%async_computation.11 | async-start | bytes 1179648 | tf_op jit(solution)/shard_map/all_gather | solution.py:80
  48.6 35.7 %copy-start.22 = (s32[64]{0:T(128)}, s32[64]{0:T(128)S(1)}, u32[]{:S(2)}) copy-start(s32[64]{0:T(128)S(1)} %select_reduce_fusion.1) | copy-start | bytes 772
  110.5 87.6 %copy-start.4 = (bf16[3,8,4096]{2,1,0:T(8,128)(2,1)S(1)}, bf16[3,8,4096]{2,1,0:T(8,128)(2,1)}, u32[]{:S(2)}) copy-start(bf16[3,8,4096]{2,1,0:T(8,128)(2,1)} %param.16) | copy-start | bytes 589828
  110.5 87.8 %copy-start.8 = (f32[4096]{0:T(1024)S(1)}, f32[4096]{0:T(1024)}, u32[]{:S(2)}) copy-start(f32[4096]{0:T(1024)} %param.17) | copy-start | bytes 49156
  110.5 87.8 %copy-start.20 = (s32[64]{0:T(128)S(1)}, s32[64]{0:T(128)}, u32[]{:S(2)}) copy-start(s32[64]{0:T(128)} %and_select_fusion) | copy-start | bytes 772
  110.5 87.8 %copy-start.24 = (s32[64]{0:T(128)S(1)}, s32[64]{0:T(128)}, u32[]{:S(2)}) copy-start(s32[64]{0:T(128)} %multiply_add_fusion.1) | copy-start | bytes 772
  173.2 8.3 %all-to-all-start = ((bf16[8,8,512]{2,1,0:T(8,128)(2,1)}), bf16[8,8,512]{2,1,0:T(8,128)(2,1)S(1)}, u32[]{:S(2)}, u32[]{:S(2)}) async-start(bf16[8,8,512]{2,1,0:T(8,128)(2,1)} %fusion.132), calls=%async_computation | async-start | bytes 131072 | tf_op jit(solution)/shard_map/all_to_all | solution.py:87
  181.5 8.3 %all-to-all-start.3 = ((bf16[8,8,512]{2,1,0:T(8,128)(2,1)}), bf16[8,8,512]{2,1,0:T(8,128)(2,1)S(1)}, u32[]{:S(2)}, u32[]{:S(2)}) async-start(bf16[8,8,512]{2,1,0:T(8,128)(2,1)} %fusion.133), calls=%async_computation.3 | async-start | bytes 131072 | tf_op jit(solution)/shard_map/all_to_all | solution.py:87
  189.8 8.3 %all-to-all-start.6 = ((bf16[8,8,512]{2,1,0:T(8,128)(2,1)}), bf16[8,8,512]{2,1,0:T(8,128)(2,1)S(1)}, u32[]{:S(2)}, u32[]{:S(2)}) async-start(bf16[8,8,512]{2,1,0:T(8,128)(2,1)} %fusion.134), calls=%async_computation.6 | async-start | bytes 131072 | tf_op jit(solution)/shard_map/all_to_all | solution.py:87
  200.7 50.4 %all-to-all-start.4 = ((bf16[32,8,4096]{2,1,0:T(8,128)(2,1)}), bf16[32,8,4096]{2,1,0:T(8,128)(2,1)S(1)}, u32[]{:S(2)}, u32[]{:S(2)}) async-start(bf16[32,8,4096]{2,1,0:T(8,128)(2,1)} %fusion.37), calls=%async_computation.4 | async-start | bytes 4194304 | tf_op jit(solution)/shard_map/all_to_all | solution.py:118
  206.6 48.8 %copy-start.16 = (s32[1,8,8]{2,1,0:T(8,128)S(1)}, s32[1,8,8]{2,1,0:T(8,128)}, u32[]{:S(2)}) copy-start(s32[1,8,8]{2,1,0:T(8,128)} %get-tuple-element.44) | copy-start | bytes 772
  251.0 51.6 %all-to-all-start.7 = ((bf16[32,8,4096]{2,1,0:T(8,128)(2,1)}), bf16[32,8,4096]{2,1,0:T(8,128)(2,1)}, u32[]{:S(2)}, u32[]{:S(2)}) async-start(bf16[32,8,4096]{2,1,0:T(8,128)(2,1)} %fusion.38), calls=%async_computation.7 | async-start | bytes 4194304 | tf_op jit(solution)/shard_map/all_to_all | solution.py:118
  302.7 51.8 %all-to-all-start.1 = ((bf16[32,8,4096]{2,1,0:T(8,128)(2,1)}), bf16[32,8,4096]{2,1,0:T(8,128)(2,1)}, u32[]{:S(2)}, u32[]{:S(2)}) async-start(bf16[32,8,4096]{2,1,0:T(8,128)(2,1)} %fusion.36), calls=%async_computation.1 | async-start | bytes 4194304 | tf_op jit(solution)/shard_map/all_to_all | solution.py:118
  354.4 51.9 %all-to-all-start.5 = ((bf16[32,8,4096]{2,1,0:T(8,128)(2,1)}), bf16[32,8,4096]{2,1,0:T(8,128)(2,1)S(1)}, u32[]{:S(2)}, u32[]{:S(2)}) async-start(bf16[32,8,4096]{2,1,0:T(8,128)(2,1)} %fusion.30), calls=%async_computation.5 | async-start | bytes 4194304 | tf_op jit(solution)/shard_map/all_to_all | solution.py:126
  406.3 51.3 %all-to-all-start.8 = ((bf16[32,8,4096]{2,1,0:T(8,128)(2,1)}), bf16[32,8,4096]{2,1,0:T(8,128)(2,1)}, u32[]{:S(2)}, u32[]{:S(2)}) async-start(bf16[32,8,4096]{2,1,0:T(8,128)(2,1)} %fusion.27), calls=%async_computation.8 | async-start | bytes 4194304 | tf_op jit(solution)/shard_map/all_to_all | solution.py:126
  428.0 34.3 %copy-start.15 = (s32[1,8,8]{2,1,0:T(8,128)S(1)}, s32[1,8,8]{2,1,0:T(8,128)}, u32[]{:S(2)}) copy-start(s32[1,8,8]{2,1,0:T(8,128)} %get-tuple-element.42) | copy-start | bytes 772
  428.0 34.4 %copy-start.14 = (s32[1,8,8]{2,1,0:T(8,128)S(1)}, s32[1,8,8]{2,1,0:T(8,128)}, u32[]{:S(2)}) copy-start(s32[1,8,8]{2,1,0:T(8,128)} %get-tuple-element.43) | copy-start | bytes 772
  428.0 34.5 %copy-start.13 = (s32[1,8,8]{2,1,0:T(8,128)S(1)}, s32[1,8,8]{2,1,0:T(8,128)}, u32[]{:S(2)}) copy-start(s32[1,8,8]{2,1,0:T(8,128)} %get-tuple-element.41) | copy-start | bytes 772
  428.0 34.6 %copy-start.23 = (s32[64]{0:T(128)S(1)}, s32[64]{0:T(128)}, u32[]{:S(2)}) copy-start(s32[64]{0:T(128)} %copy-done.22) | copy-start | bytes 772
  428.0 34.6 %copy-start.11 = (f32[3,8,8]{2,1,0:T(8,128)S(1)}, f32[3,8,8]{2,1,0:T(8,128)}, u32[]{:S(2)}) copy-start(f32[3,8,8]{2,1,0:T(8,128)} %param.20) | copy-start | bytes 2308
  457.5 52.1 %all-to-all-start.2 = ((bf16[32,8,4096]{2,1,0:T(8,128)(2,1)}), bf16[32,8,4096]{2,1,0:T(8,128)(2,1)}, u32[]{:S(2)}, u32[]{:S(2)}) async-start(bf16[32,8,4096]{2,1,0:T(8,128)(2,1)} %fusion.33), calls=%async_computation.2 | async-start | bytes 4194304 | tf_op jit(solution)/shard_map/all_to_all | solution.py:126
  (15 other events, 70.3 us)
Sparse Core Ops, SparseCore 0:
  30.8 26.1 all-gather.3
  58.9 23.4 all-gather.5
  84.3 23.4 all-gather.7
where the time goes:
time: 525 us; the launch traced here: 523 us
  waiting for transfers between devices  289 us (55%)
  matrix products  77.3 us (15%)
  blocking collectives  61.5 us (12%)
  starting transfers between devices  35.3 us (7%)
  local copies, waits for them, and re-layouts  30.1 us (6%)
  other arithmetic  16.3 us (3%)
  between operations  13.7 us (3%)
    all_to_all x3, waiting for transfers between devices, per_device(): lax.all_to_all(outgoing, ('ep', 'tp'), split_axis=0, concat_axis=0, tiled...  120 us
    all_to_all x3, waiting for transfers between devices, per_device(): lax.all_to_all(expert_out.reshape(arrived.shape), ('ep', 'tp'), split_axi...  101 us
    unnamed x1, blocking collectives  61.5 us
    all_gather x3, waiting for transfers between devices, per_device(): lax.all_gather(attended, 'ep', axis=0, tiled=True)  54.7 us
    dot_general x3, matrix products, per_device(): jnp.dot(hidden, down_weights, preferred_element_type=jnp.float32)  33.3 us
    dot_general x3, matrix products, per_device(): jnp.dot(flat_rows, gate_weights, preferred_element_type=jnp.float32)  17.8 us
    all_to_all x3, starting transfers between devices, per_device(): lax.all_to_all(expert_out.reshape(arrived.shape), ('ep', 'tp'), split_axi...  13.4 us
    all_to_all x3, waiting for transfers between devices, per_device(): lax.all_to_all(projected, 'ep', split_axis=0, concat_axis=2, tiled=True)  12.4 us
  transfers between devices with their start and end apart: 12, of which 12 were waited for; matrix products, arithmetic and copies ran while one was open for 17% of the time, Pallas kernels for 0%

commit v1 on v0

v1 whole, which is shorter than its diff:
```python
import jax
import jax.numpy as jnp
from jax import lax
from jax.sharding import PartitionSpec as P

HEAD_SIZE = 128
GROUPS = ((0, 1, 2),)

masked_score = -1e30
norm_eps = 1e-06


def attend(query, step_key_value, key_value_cache, lengths):
    steps, row_dev, columns = query.shape
    heads_dev = columns // HEAD_SIZE
    cache_len = key_value_cache.shape[2]
    score_scale = HEAD_SIZE ** (-0.5)
    rows = query.reshape(steps, row_dev, heads_dev, HEAD_SIZE).transpose(1, 0, 2, 3)
    rows = rows.reshape(row_dev, steps * heads_dev, HEAD_SIZE)
    fresh = step_key_value.transpose(1, 2, 0, 3)
    usable = jnp.arange(cache_len, dtype=jnp.int32)[None, :] < lengths[:, None]
    cache_scores = (
        jnp.einsum("rhd,rjd->rhj", rows, key_value_cache[0], preferred_element_type=jnp.float32)
        * score_scale
    )
    cache_scores = jnp.where(usable[:, None, :], cache_scores, masked_score)
    fresh_scores = (
        jnp.einsum("rhd,rjd->rhj", rows, fresh[0], preferred_element_type=jnp.float32)
        * score_scale
    )
    step_of = jnp.arange(steps * heads_dev, dtype=jnp.int32) // heads_dev
    known = jnp.arange(steps, dtype=jnp.int32)[None, :] <= step_of[:, None]
    fresh_scores = jnp.where(known[None], fresh_scores, masked_score)
    top = jnp.maximum(
        jnp.max(cache_scores, axis=-1, keepdims=True), jnp.max(fresh_scores, axis=-1, keepdims=True)
    )
    cache_raised = jnp.exp(cache_scores - top)
    fresh_raised = jnp.exp(fresh_scores - top)
    total = jnp.sum(cache_raised, axis=-1, keepdims=True) + jnp.sum(
        fresh_raised, axis=-1, keepdims=True
    )
    cache_probs = (cache_raised / total).astype(jnp.bfloat16)
    fresh_probs = (fresh_raised / total).astype(jnp.bfloat16)
    attended = jnp.einsum(
        "rhj,rjd->rhd", cache_probs, key_value_cache[1], preferred_element_type=jnp.float32
    ) + jnp.einsum("rhj,rjd->rhd", fresh_probs, fresh[1], preferred_element_type=jnp.float32)
    attended = attended.astype(jnp.bfloat16).reshape(row_dev, steps, heads_dev * HEAD_SIZE)
    return attended.transpose(1, 0, 2)


def per_device(
    query,
    step_key_value,
    key_value_cache,
    lengths,
    hidden_in,
    norm_gain,
    w_out,
    routes,
    gate_scores,
    expert_gate,
    expert_up,
    expert_down,
):
    ep_count = lax.axis_size("ep")
    tp_count = lax.axis_size("tp")
    row_own = hidden_in.shape[1]
    width = hidden_in.shape[2]
    cols = w_out.shape[1]
    expert_count = ep_count * tp_count * expert_gate.shape[0]
    mine = lax.axis_index("ep") * tp_count + lax.axis_index("tp")

    weights = gate_scores / jnp.sum(gate_scores, axis=-1, keepdims=True)
    named = routes[..., None] == jnp.arange(expert_count, dtype=jnp.int32)
    dense = jnp.sum(jnp.where(named, weights[..., None], 0.0), axis=2)

    attended = attend(query, step_key_value, key_value_cache, lengths)
    results = []
    for group in GROUPS:
        first, count = group[0], len(group)
        group_dense = dense[first : first + count].reshape(count * row_own, expert_count)
        all_dense = lax.all_gather(group_dense, ("ep", "tp"), axis=0, tiled=True)
        my_weight = lax.dynamic_slice_in_dim(all_dense, mine, 1, axis=1)

        part = attended[first : first + count]
        row_dev = part.shape[1]
        everyone = lax.all_gather(part.reshape(count * row_dev, -1), "ep", axis=0, tiled=True)
        partial_sums = jnp.dot(everyone, w_out, preferred_element_type=jnp.float32)
        grouped = partial_sums.reshape(ep_count, count, tp_count, row_own, cols)
        grouped = grouped.transpose(2, 0, 1, 3, 4).reshape(tp_count * ep_count * count * row_own, cols)
        summed = lax.psum_scatter(grouped, "tp", scatter_dimension=0, tiled=True)
        projected = summed.reshape(ep_count, count * row_own, cols).astype(jnp.bfloat16)
        row_major = lax.all_to_all(
            projected, "ep", split_axis=0, concat_axis=2, tiled=True
        ).reshape(count * row_own, width)
        own = hidden_in[first : first + count].reshape(count * row_own, width)
        residual = own.astype(jnp.float32) + row_major.astype(jnp.float32)
        mean_square = jnp.mean(residual * residual, axis=-1, keepdims=True)
        normed = (residual * lax.rsqrt(mean_square + norm_eps) * norm_gain).astype(jnp.bfloat16)

        flat_rows = lax.all_gather(normed, ("ep", "tp"), axis=0, tiled=True)
        gate_act = jnp.dot(flat_rows, expert_gate[0], preferred_element_type=jnp.float32)
        up_act = jnp.dot(flat_rows, expert_up[0], preferred_element_type=jnp.float32)
        hidden = (jax.nn.silu(gate_act) * up_act).astype(jnp.bfloat16)
        expert_out = jnp.dot(hidden, expert_down[0], preferred_element_type=jnp.float32).astype(
            jnp.bfloat16
        )
        share = (expert_out.astype(jnp.float32) * my_weight).astype(jnp.bfloat16)
        mix = lax.psum_scatter(share, ("ep", "tp"), scatter_dimension=0, tiled=True)
        layer_out = (residual + mix.astype(jnp.float32)).astype(jnp.bfloat16)
        results.append(layer_out.reshape(count, row_own, width))
    return jnp.concatenate(results) if len(results) > 1 else results[0]


def solution(mesh):
    placed = (
        P(None, "ep", "tp"),
        P(None, None, "ep", "tp"),
        P(None, "ep", None, "tp"),
        P("ep"),
        P(None, ("ep", "tp"), None),
        P(),
        P("tp", "ep"),
        P(None, ("ep", "tp"), None),
        P(None, ("ep", "tp"), None),
        P(("ep", "tp"), None, None),
        P(("ep", "tp"), None, None),
        P(("ep", "tp"), None, None),
    )
    return jax.shard_map(
        per_device,
        mesh=mesh,
        in_specs=placed,
        out_specs=P(None, ("ep", "tp"), None),
        check_vma=False,
    )
```

time: 525 us -> 321 us (0.61)
  waiting for transfers between devices: 289 us -> 182 us
  matrix products: 77.3 us -> 34.2 us
  starting transfers between devices: 35.3 us -> 0.13 us
  local copies, waits for them, and re-layouts: 30.1 us -> 5.37 us
  blocking collectives: 61.5 us -> 80.2 us
  other arithmetic: 16.3 us -> 5.44 us
    all_to_all x9 -> x0, waiting for transfers between devices: 234 us -> none  [the longest x3 120 us: per_device(): lax.all_to_all(outgoing, ('ep', 'tp'), split_axis=0, concat_axis=0, tiled...]
    reduce_scatter x0 -> x2, waiting for transfers between devices: none -> 147 us  [the longest x1 111 us: per_device(): mix = lax.psum_scatter(share, ('ep', 'tp'), scatter_dimension=0, tiled=True)]
    all_gather x0 -> x1, blocking collectives: none -> 70.5 us  [per_device(): all_dense = lax.all_gather(group_dense, ('ep', 'tp'), axis=0, tiled=True)]
    unnamed x1 -> x0, blocking collectives: 61.5 us -> none
    dot_general x23 -> x8, matrix products: 77.3 us -> 34.2 us  [the longest x1 9.82 us: per_device(): jnp.dot(hidden, expert_down[0], preferred_element_type=jnp.float32)]
    all_to_all x9 -> x0, starting transfers between devices: 35.2 us -> none  [the longest x3 13.4 us: per_device(): lax.all_to_all(expert_out.reshape(arrived.shape), ('ep', 'tp'), split_axi...]
    all_gather x3 -> x2, waiting for transfers between devices: 54.7 us -> 35.1 us  [the longest x1 35.1 us: per_device(): lax.all_gather(part.reshape(count * row_dev, -1), 'ep', axis=0, tiled=True)]
    all_to_all x0 -> x1, blocking collectives: none -> 9.67 us  [per_device(): lax.all_to_all(projected, 'ep', split_axis=0, concat_axis=2, tiled=True)]
  transfers between devices with their start and end apart: 12 -> 4, of which waited for: 12 -> 3; matrix products, arithmetic and copies ran while one was open for 17% -> 0% of each run, Pallas kernels for 0% -> 0%
where the time goes in v1:
time: 321 us
  waiting for transfers between devices  182 us (57%)
  blocking collectives  80.2 us (25%)
  matrix products  34.2 us (11%)
  between operations  13.4 us (4%)
  other arithmetic  5.44 us (2%)
  local copies, waits for them, and re-layouts  5.37 us (2%)
    reduce_scatter x1, waiting for transfers between devices, per_device(): mix = lax.psum_scatter(share, ('ep', 'tp'), scatter_dimension=0, tiled=True)  111 us
    all_gather x1, blocking collectives, per_device(): all_dense = lax.all_gather(group_dense, ('ep', 'tp'), axis=0, tiled=True)  70.5 us
    reduce_scatter x1, waiting for transfers between devices, per_device(): summed = lax.psum_scatter(grouped, 'tp', scatter_dimension=0, tiled=True)  35.4 us
    all_gather x1, waiting for transfers between devices, per_device(): lax.all_gather(part.reshape(count * row_dev, -1), 'ep', axis=0, tiled=True)  35.1 us
    dot_general x1, matrix products, per_device(): jnp.dot(hidden, expert_down[0], preferred_element_type=jnp.float32)  9.82 us
    all_to_all x1, blocking collectives, per_device(): lax.all_to_all(projected, 'ep', split_axis=0, concat_axis=2, tiled=True)  9.67 us
    dot_general x1, matrix products, per_device(): jnp.dot(flat_rows, expert_gate[0], preferred_element_type=jnp.float32)  9.11 us
    dot_general x1, matrix products, per_device(): jnp.dot(flat_rows, expert_up[0], preferred_element_type=jnp.float32)  8.02 us
  transfers between devices with their start and end apart: 4, of which 3 were waited for; matrix products, arithmetic and copies ran while one was open for 0% of the time, Pallas kernels for 0%

profile of v1, /device:TPU:0, one launch (start us, length us, event | category | flops | bytes accessed | tf_op | source)
XLA Modules:
  0.0 320.7 jit_solution(5914425658996849807)
XLA Ops:
  6.5 1.2 copy.32
  7.8 0.9 copy.36
  8.8 0.7 iota_compare_fusion.1
  9.5 0.3 fusion.30
  9.8 2.1 fusion.29
  12.0 0.5 fusion.17
  12.6 0.8 fusion.12
  13.4 0.3 fusion.10
  13.9 1.0 copy.28
  15.0 35.1 %all-gather.3.cloned.1.call-done = bf16[768,2048]{1,0:T(8,128)(2,1)} async-done(((bf16[96,2048]{1,0:T(8,128)(2,1)}), bf16[768,2048]{1,0:T(8,128)(2,1)}) %all-gather.3.cloned.1.call-update) | async-done | bytes 3145744 | tf_op jit(solution)/shard_map/all_gather | solution.py:87
  50.1 3.7 %fusion.32 = f32[768,512]{1,0:T(8,128)S(1)} fusion(bf16[768,2048]{1,0:T(8,128)(2,1)} %all-gather.3.cloned.1.call-done, bf16[2048,512]{1,0:T(8,128)(2,1)S(1)} %copy-done), kind=kOutput, calls=%fused_computation.57 | convolution fusion | flops 1610612736 | bytes 6815744 | tf_op jit(solution)/shard_map/dot_general | solution.py:88
  53.8 1.3 copy.29
  55.2 35.4 %reduce-scatter.3.cloned.1.call-done = f32[192,512]{1,0:T(8,128)} async-done(((f32[768,512]{1,0:T(8,128)}), f32[192,512]{1,0:T(8,128)}) %reduce-scatter.3.cloned.1.call-update) | async-done | bytes 393232 | tf_op jit(solution)/shard_map/reduce_scatter | solution.py:91
  90.6 1.0 convert_element_type.70
  91.6 9.7 %all_to_all.4 = bf16[8,24,512]{2,1,0:T(8,128)(2,1)S(1)} all-to-all(bf16[8,24,512]{2,1,0:T(8,128)(2,1)S(1)} %bitcast.94), channel_id=1, replica_groups=mesh['ep'=8,'tp'=4] {'ep'}, dimensions={0} | all-to-all | bytes 393216 | tf_op jit(solution)/shard_map/all_to_all | solution.py:93
  102.0 0.8 multiply_convert_fusion.2
  102.9 0.3 fusion.28
  103.3 70.5 %all_gather.11 = f32[768,32]{1,0:T(8,128)S(1)} all-gather(f32[24,32]{1,0:T(8,128)S(1)} %bitcast.98), channel_id=1, replica_groups=mesh['ep'=8,'tp'=4] {'ep','tp'}, dimensions={0}, use_global_device_ids=true | all-gather | bytes 101376 | tf_op jit(solution)/shard_map/all_gather | solution.py:82
  173.8 0.3 dynamic-slice_reduce_fusion
  174.1 9.1 %fusion.3 = f32[768,768]{1,0:T(8,128)S(1)} fusion(bf16[768,4096]{1,0:T(8,128)(2,1)} %all-gather.5.cloned.1.call-done, bf16[1,4096,768]{2,1,0:T(8,128)(2,1)} %param.21), kind=kOutput, calls=%fused_computation.5 | convolution fusion | flops 4831838208 | bytes 14942208 | tf_op jit(solution)/shard_map/dot_general | solution.py:102
  183.3 8.0 %multiply_convert_fusion.1 = bf16[768,768]{1,0:T(8,128)(2,1)S(1)} fusion(f32[768,768]{1,0:T(8,128)S(1)} %fusion.3, bf16[768,4096]{1,0:T(8,128)(2,1)S(1)} %copy-done.5, bf16[1,4096,768]{2,1,0:T(8,128)(2,1)} %param.22), kind=kOutput, calls=%fused_computation.7 | convolution fusion | flops 4835377152 | bytes 16121856 | tf_op jit(solution)/shard_map/dot_general | solution.py:103
  191.3 9.8 %multiply_convert_fusion = bf16[768,4096]{1,0:T(8,128)(2,1)} fusion(f32[768]{0:T(1024)S(1)} %dynamic-slice_reduce_fusion, bf16[768,768]{1,0:T(8,128)(2,1)S(1)} %multiply_convert_fusion.1, bf16[1,768,4096]{2,1,0:T(8,128)(2,1)} %param.23), kind=kOutput, calls=%fused_computation | convolution fusion | flops 4844421120 | bytes 13765632 | tf_op jit(solution)/shard_map/dot_general | solution.py:105
  201.1 111.4 %reduce-scatter.5.cloned.1.call-done = bf16[24,4096]{1,0:T(8,128)(2,1)} async-done(((bf16[768,4096]{1,0:T(8,128)(2,1)}), bf16[24,4096]{1,0:T(8,128)(2,1)}) %reduce-scatter.5.cloned.1.call-update) | async-done | bytes 196624 | tf_op jit(solution)/shard_map/reduce_scatter | solution.py:109
  312.5 1.7 fusion.23
  (40 shorter events, 1.3 us)
Async XLA Ops:
  6.5 43.6 %copy-start = (bf16[2048,512]{1,0:T(8,128)(2,1)S(1)}, bf16[2048,512]{1,0:T(8,128)(2,1)}, u32[]{:S(2)}) copy-start(bf16[2048,512]{1,0:T(8,128)(2,1)} %param.18) | copy-start | bytes 6291460
  6.5 43.6 %all-gather.3.cloned.1.call-start = ((), (), s32[]{:S(2)}) async-start(), calls=%async_computation.3 | async-start | bytes 3538944 | tf_op jit(solution)/shard_map/all_gather | solution.py:87
  6.5 6.0 %copy-start.2 = (bf16[2,32,128,128]{3,2,1,0:T(8,128)(2,1)S(1)}, bf16[2,32,128,128]{3,2,1,0:T(8,128)(2,1)}, u32[]{:S(2)}) copy-start(bf16[2,32,128,128]{3,2,1,0:T(8,128)(2,1)} %param.14) | copy-start | bytes 6291460
  14.9 75.6 %reduce-scatter.3.cloned.1.call-start = ((), (), s32[]{:S(2)}) async-start(), calls=%async_computation.4 | async-start | bytes 1966080 | tf_op jit(solution)/shard_map/reduce_scatter | solution.py:91
  55.1 46.6 %copy-start.1 = (bf16[3,8,4096]{2,1,0:T(8,128)(2,1)S(1)}, bf16[3,8,4096]{2,1,0:T(8,128)(2,1)}, u32[]{:S(2)}) copy-start(bf16[3,8,4096]{2,1,0:T(8,128)(2,1)} %param.16) | copy-start | bytes 589828
  55.1 46.9 %copy-start.3 = (f32[4096]{0:T(1024)S(1)}, f32[4096]{0:T(1024)}, u32[]{:S(2)}) copy-start(f32[4096]{0:T(1024)} %param.17) | copy-start | bytes 49156
  55.1 47.7 %copy-start.6 = (f32[3,8,8]{2,1,0:T(8,128)S(1)}, f32[3,8,8]{2,1,0:T(8,128)}, u32[]{:S(2)}) copy-start(f32[3,8,8]{2,1,0:T(8,128)} %param.20) | copy-start | bytes 2308
  55.1 48.0 %copy-start.4 = (s32[3,8,8]{2,1,0:T(8,128)S(1)}, s32[3,8,8]{2,1,0:T(8,128)}, u32[]{:S(2)}) copy-start(s32[3,8,8]{2,1,0:T(8,128)} %param.19) | copy-start | bytes 2308
  55.2 119.0 %all-gather.5.cloned.1.call-start = ((), (), s32[]{:S(2)}) async-start(), calls=%async_computation.5 | async-start | bytes 6488064 | tf_op jit(solution)/shard_map/all_gather | solution.py:101
  102.8 209.7 %reduce-scatter.5.cloned.1.call-start = ((), (), s32[]{:S(2)}) async-start(), calls=%async_computation.6 | async-start | bytes 6488064 | tf_op jit(solution)/shard_map/reduce_scatter | solution.py:109
  174.1 9.1 %copy-start.5 = (bf16[768,4096]{1,0:T(8,128)(2,1)S(1)}, bf16[768,4096]{1,0:T(8,128)(2,1)}, u32[]{:S(2)}) copy-start(bf16[768,4096]{1,0:T(8,128)(2,1)} %all-gather.5.cloned.1.call-done) | copy-start | bytes 18874372
Sparse Core Ops, SparseCore 0:
  15.1 35.0 all-gather.2
  55.2 35.2 reduce-scatter.2
  102.9 67.7 all-gather.4
  201.3 111.2 reduce-scatter.4

commit v2 on v1

v2 whole, which is shorter than its diff:
```python
import functools

import jax
import jax.numpy as jnp
from jax import lax
from jax.experimental import pallas as pl
from jax.experimental.pallas import tpu as pltpu
from jax.sharding import PartitionSpec as P

HEAD_SIZE = 128
CHUNKS = 4
MESH = pl.DeviceIdType.MESH

masked_score = -1e30
norm_eps = 1e-06


def greet(devices):
    barrier = pltpu.get_barrier_semaphore()
    for device in devices:
        pl.semaphore_signal(barrier, inc=1, device_id=device, device_id_type=MESH)
    pl.semaphore_wait(barrier, len(devices))


def gather_kernel(chips, depth, x_ref, out_ref, own_sem, z_send, z_recv, c_send, c_recv, p_send, p_recv):
    ep, tp = lax.axis_index("ep"), lax.axis_index("tp")
    chip, core = ep // 2, ep % 2
    partner = (chip * 2 + 1 - core, tp)
    chip_of = [(chip + j) % chips for j in range(chips)]
    chip_from = [(chip + chips - j) % chips for j in range(chips)]
    if depth > 1:
        tp_of = [(tp + t) % depth for t in range(depth)]
        tp_from = [(tp + depth - t) % depth for t in range(depth)]
    else:
        tp_from = [0]
    greet(
        [partner]
        + [(chip_of[j] * 2 + core, tp) for j in range(1, chips)]
        + [(ep, tp_of[t]) for t in range(1, depth)]
    )

    def push(src, slot, send, recv, device):
        copy = pltpu.make_async_remote_copy(
            src_ref=src,
            dst_ref=out_ref.at[slot],
            send_sem=send,
            recv_sem=recv,
            device_id=device,
            device_id_type=MESH,
        )
        copy.start()
        return copy

    def arrival(slot, recv):
        pltpu.make_async_remote_copy(
            src_ref=out_ref.at[slot],
            dst_ref=out_ref.at[slot],
            send_sem=recv,
            recv_sem=recv,
            device_id=partner,
            device_id_type=MESH,
        ).wait_recv()

    sent = []
    own_slot = (chip, core, tp_from[0])
    for t in range(1, depth):
        sent.append(push(x_ref, own_slot, z_send.at[t], z_recv.at[t], (ep, tp_of[t])))
    own = pltpu.make_async_copy(x_ref, out_ref.at[own_slot], own_sem)
    own.start()
    for t in range(depth):
        slot = (chip, core, tp_from[t])
        src = x_ref
        if t > 0:
            arrival(slot, z_recv.at[t])
            src = out_ref.at[slot]
        for j in range(chips - 1, 0, -1):
            device = (chip_of[j] * 2 + core, tp)
            sent.append(push(src, slot, c_send.at[t, j], c_recv.at[t, j], device))
        sent.append(push(src, slot, p_send.at[t, 0], p_recv.at[t, 0], partner))
    for t in range(depth):
        for j in range(1, chips):
            slot = (chip_from[j], core, tp_from[t])
            arrival(slot, c_recv.at[t, j])
            sent.append(push(out_ref.at[slot], slot, p_send.at[t, j], p_recv.at[t, j], partner))
    for t in range(depth):
        for j in range(chips):
            arrival((chip_from[j], 1 - core, tp_from[t]), p_recv.at[t, j])
    own.wait()
    for copy in sent:
        copy.wait_send()


def gather(x, chips, depth, collective_id):
    rows, columns = x.shape
    dma = pltpu.SemaphoreType.DMA
    return pl.pallas_call(
        functools.partial(gather_kernel, chips, depth),
        out_shape=jax.ShapeDtypeStruct((chips, 2, depth, rows, columns), x.dtype),
        in_specs=[pl.BlockSpec(memory_space=pl.ANY)],
        out_specs=pl.BlockSpec(memory_space=pl.ANY),
        scratch_shapes=[
            dma,
            dma((depth,)),
            dma((depth,)),
            dma((depth, chips)),
            dma((depth, chips)),
            dma((depth, chips)),
            dma((depth, chips)),
        ],
        compiler_params=pltpu.CompilerParams(collective_id=collective_id, has_side_effects=True),
    )(x).reshape(chips * 2 * depth * rows, columns)


def scatter_kernel(
    chips,
    depth,
    share_ref,
    residual_ref,
    out_ref,
    own,
    from_core,
    from_chips,
    mid,
    from_z,
    kept,
    own_sem,
    p_send,
    p_recv,
    c_send,
    c_recv,
    z_send,
    z_recv,
):
    ep, tp = lax.axis_index("ep"), lax.axis_index("tp")
    chip, core = ep // 2, ep % 2
    partner = (chip * 2 + 1 - core, tp)
    chip_of = [(chip + j) % chips for j in range(chips)]
    tp_of = [(tp + t) % depth for t in range(depth)]
    peers = [(chip_of[j] * 2 + core, tp) for j in range(chips)]
    layers = [(ep, tp_of[t]) for t in range(depth)]
    greet([partner] + peers[1:] + layers[1:])
    part = own.shape[-1]
    order = list(range(chips - 1, -1, -1))

    def columns(k):
        return pl.ds(k * part, part)

    def to_core(k, j):
        return pltpu.make_async_remote_copy(
            src_ref=share_ref.at[chip_of[j], 1 - core, :, :, columns(k)],
            dst_ref=from_core.at[k, j],
            send_sem=p_send.at[k, j],
            recv_sem=p_recv.at[k, j],
            device_id=partner,
            device_id_type=MESH,
        )

    def load(k, j):
        return pltpu.make_async_copy(
            share_ref.at[chip_of[j], core, :, :, columns(k)], own.at[k, j], own_sem.at[k, j]
        )

    def to_chip(k, j):
        return pltpu.make_async_remote_copy(
            src_ref=own.at[k, j],
            dst_ref=from_chips.at[k, j],
            send_sem=c_send.at[k, j],
            recv_sem=c_recv.at[k, j],
            device_id=peers[j],
            device_id_type=MESH,
        )

    def to_layer(k, t):
        return pltpu.make_async_remote_copy(
            src_ref=mid.at[k, t],
            dst_ref=from_z.at[k, t],
            send_sem=z_send.at[k, t],
            recv_sem=z_recv.at[k, t],
            device_id=layers[t],
            device_id_type=MESH,
        )

    def over_chips(k):
        for j in range(1, chips):
            to_chip(k, j).wait_recv()
        for t in list(range(1, depth)) + [0]:
            total = own[k, 0, tp_of[t]].astype(jnp.float32)
            for j in range(1, chips):
                total += from_chips[k, j, tp_of[t]].astype(jnp.float32)
            if t > 0:
                mid[k, t] = total.astype(mid.dtype)
                to_layer(k, t).start()
            else:
                kept[k] = total

    def finish(k):
        total = kept[k] + residual_ref[:, columns(k)]
        for t in range(1, depth):
            to_layer(k, t).wait_recv()
            total += from_z[k, t].astype(jnp.float32)
        out_ref[:, columns(k)] = total.astype(out_ref.dtype)

    for k in range(CHUNKS):
        for j in order:
            to_core(k, j).start()
            load(k, j).start()
    for k in range(CHUNKS):
        for j in order:
            to_core(k, j).wait_recv()
            load(k, j).wait()
            for t in range(depth):
                own[k, j, t] = (
                    own[k, j, t].astype(jnp.float32) + from_core[k, j, t].astype(jnp.float32)
                ).astype(own.dtype)
            if j > 0:
                to_chip(k, j).start()
        if k > 0:
            over_chips(k - 1)
    over_chips(CHUNKS - 1)
    for k in range(CHUNKS):
        finish(k)
    for k in range(CHUNKS):
        for j in range(chips):
            to_core(k, j).wait_send()
            if j > 0:
                to_chip(k, j).wait_send()
        for t in range(1, depth):
            to_layer(k, t).wait_send()


def scatter(share, residual, chips, depth, collective_id):
    rows, width = residual.shape
    part = width // CHUNKS
    dma = pltpu.SemaphoreType.DMA
    vmem = pltpu.VMEM
    blocks = (CHUNKS, chips, depth, rows, part)
    return pl.pallas_call(
        functools.partial(scatter_kernel, chips, depth),
        out_shape=jax.ShapeDtypeStruct((rows, width), jnp.bfloat16),
        in_specs=[
            pl.BlockSpec(memory_space=pl.ANY),
            pl.BlockSpec(memory_space=pltpu.VMEM),
        ],
        out_specs=pl.BlockSpec(memory_space=pltpu.VMEM),
        scratch_shapes=[
            vmem(blocks, jnp.bfloat16),
            vmem(blocks, jnp.bfloat16),
            vmem(blocks, jnp.bfloat16),
            vmem((CHUNKS, depth, rows, part), jnp.bfloat16),
            vmem((CHUNKS, depth, rows, part), jnp.bfloat16),
            vmem((CHUNKS, rows, part), jnp.float32),
            dma((CHUNKS, chips)),
            dma((CHUNKS, chips)),
            dma((CHUNKS, chips)),
            dma((CHUNKS, chips)),
            dma((CHUNKS, chips)),
            dma((CHUNKS, depth)),
            dma((CHUNKS, depth)),
        ],
        compiler_params=pltpu.CompilerParams(
            collective_id=collective_id, has_side_effects=True, vmem_limit_bytes=56 * 1024 * 1024
        ),
    )(share.reshape(chips, 2, depth, rows, width), residual)


def attend(query, step_key_value, key_value_cache, lengths, owners):
    steps, row_dev, columns = query.shape
    heads_dev = columns // HEAD_SIZE
    cache_len = key_value_cache.shape[2]
    score_scale = HEAD_SIZE ** (-0.5)
    rows = query.reshape(steps, row_dev, heads_dev, HEAD_SIZE).transpose(1, 0, 2, 3)
    rows = rows.reshape(row_dev, steps * heads_dev, HEAD_SIZE)
    fresh = step_key_value.transpose(1, 2, 0, 3)
    usable = jnp.arange(cache_len, dtype=jnp.int32)[None, :] < lengths[:, None]
    cache_scores = (
        jnp.einsum("rhd,rjd->rhj", rows, key_value_cache[0], preferred_element_type=jnp.float32)
        * score_scale
    )
    cache_scores = jnp.where(usable[:, None, :], cache_scores, masked_score)
    fresh_scores = (
        jnp.einsum("rhd,rjd->rhj", rows, fresh[0], preferred_element_type=jnp.float32)
        * score_scale
    )
    step_of = jnp.arange(steps * heads_dev, dtype=jnp.int32) // heads_dev
    known = jnp.arange(steps, dtype=jnp.int32)[None, :] <= step_of[:, None]
    fresh_scores = jnp.where(known[None], fresh_scores, masked_score)
    top = jnp.maximum(
        jnp.max(cache_scores, axis=-1, keepdims=True), jnp.max(fresh_scores, axis=-1, keepdims=True)
    )
    cache_raised = jnp.exp(cache_scores - top)
    fresh_raised = jnp.exp(fresh_scores - top)
    total = jnp.sum(cache_raised, axis=-1, keepdims=True) + jnp.sum(
        fresh_raised, axis=-1, keepdims=True
    )
    cache_probs = (cache_raised / total).astype(jnp.bfloat16)
    fresh_probs = (fresh_raised / total).astype(jnp.bfloat16)
    attended = jnp.einsum(
        "rhj,rjd->rhd", cache_probs, key_value_cache[1], preferred_element_type=jnp.float32
    ) + jnp.einsum("rhj,rjd->rhd", fresh_probs, fresh[1], preferred_element_type=jnp.float32)
    attended = attended.astype(jnp.bfloat16).reshape(owners, row_dev // owners, steps, columns)
    return attended.transpose(0, 2, 1, 3).reshape(steps * row_dev, columns)


def per_device(
    query,
    step_key_value,
    key_value_cache,
    lengths,
    hidden_in,
    norm_gain,
    w_out,
    routes,
    gate_scores,
    expert_gate,
    expert_up,
    expert_down,
):
    ep_count = lax.axis_size("ep")
    tp_count = lax.axis_size("tp")
    chips = ep_count // 2
    steps, row_own = hidden_in.shape[:2]
    width = hidden_in.shape[2]
    cols = w_out.shape[1]
    expert_count = ep_count * tp_count * expert_gate.shape[0]
    mine = lax.axis_index("ep") * tp_count + lax.axis_index("tp")

    weights = gate_scores / jnp.sum(gate_scores, axis=-1, keepdims=True)
    named = routes[..., None] == jnp.arange(expert_count, dtype=jnp.int32)
    dense = jnp.sum(jnp.where(named, weights[..., None], 0.0), axis=2)

    all_dense = lax.all_gather(
        dense.reshape(steps * row_own, expert_count), ("ep", "tp"), axis=0, tiled=True
    )
    my_weight = lax.dynamic_slice_in_dim(all_dense, mine, 1, axis=1)

    attended = attend(query, step_key_value, key_value_cache, lengths, tp_count)
    everyone = gather(attended, chips, 1, 1)
    partial_sums = jnp.dot(everyone, w_out, preferred_element_type=jnp.float32)
    partial_sums = partial_sums.astype(jnp.bfloat16).reshape(-1, steps * row_own, cols)
    arrived = lax.all_to_all(partial_sums, ("ep", "tp"), split_axis=0, concat_axis=0, tiled=True)
    arrived = arrived.reshape(ep_count, tp_count, steps * row_own, cols)
    projected = jnp.sum(arrived.astype(jnp.float32), axis=1).astype(jnp.bfloat16)
    row_major = projected.transpose(1, 0, 2).reshape(steps * row_own, width)
    own = hidden_in.reshape(steps * row_own, width)
    residual = own.astype(jnp.float32) + row_major.astype(jnp.float32)
    mean_square = jnp.mean(residual * residual, axis=-1, keepdims=True)
    normed = (residual * lax.rsqrt(mean_square + norm_eps) * norm_gain).astype(jnp.bfloat16)

    flat_rows = gather(normed, chips, tp_count, 2)
    gate_act = jnp.dot(flat_rows, expert_gate[0], preferred_element_type=jnp.float32)
    up_act = jnp.dot(flat_rows, expert_up[0], preferred_element_type=jnp.float32)
    hidden = (jax.nn.silu(gate_act) * up_act).astype(jnp.bfloat16)
    expert_out = jnp.dot(hidden, expert_down[0], preferred_element_type=jnp.float32).astype(
        jnp.bfloat16
    )
    share = (expert_out.astype(jnp.float32) * my_weight).astype(jnp.bfloat16)
    layer_out = scatter(share, residual, chips, tp_count, 3)
    return layer_out.reshape(steps, row_own, width)


def solution(mesh):
    placed = (
        P(None, "ep", "tp"),
        P(None, None, "ep", "tp"),
        P(None, "ep", None, "tp"),
        P("ep"),
        P(None, ("ep", "tp"), None),
        P(),
        P("tp", "ep"),
        P(None, ("ep", "tp"), None),
        P(None, ("ep", "tp"), None),
        P(("ep", "tp"), None, None),
        P(("ep", "tp"), None, None),
        P(("ep", "tp"), None, None),
    )
    return jax.shard_map(
        per_device,
        mesh=mesh,
        in_specs=placed,
        out_specs=P(None, ("ep", "tp"), None),
        check_vma=False,
    )
```

time: 321 us -> 243 us (0.76)
  waiting for transfers between devices: 182 us -> 0.01 us
  Pallas kernels: 0 us -> 113 us
  between operations: 13.4 us -> 0.29 us
  starting transfers between devices: 0.13 us -> 4.55 us
    reduce_scatter x2 -> x0, waiting for transfers between devices: 147 us -> none  [the longest x1 111 us: per_device(): mix = lax.psum_scatter(share, ('ep', 'tp'), scatter_dimension=0, tiled=True)]
    pallas_call x0 -> x3, Pallas kernels: none -> 113 us  [the longest x2 64.7 us: gather(): pl.pallas_call(functools.partial(gather_kernel, chips, depth), out_shape=...]
    all_gather x2 -> x0, waiting for transfers between devices: 35.1 us -> none  [the longest x1 35.1 us: per_device(): lax.all_gather(part.reshape(count * row_dev, -1), 'ep', axis=0, tiled=True)]
    all_gather x1, blocking collectives: 70.5 us -> 80.9 us  [per_device(): lax.all_gather(dense.reshape(steps * row_own, expert_count), ('ep', 'tp')...]
    all_to_all x1 -> x0, blocking collectives: 9.67 us -> none  [per_device(): lax.all_to_all(projected, 'ep', split_axis=0, concat_axis=2, tiled=True)]
    all_to_all x0 -> x1, starting transfers between devices: none -> 4.55 us  [per_device(): lax.all_to_all(partial_sums, ('ep', 'tp'), split_axis=0, concat_axis=0, t...]
  transfers between devices with their start and end apart: 4 -> 1, of which waited for: 3 -> 0; matrix products, arithmetic and copies ran while one was open for 0% -> 0% of each run, Pallas kernels for 0% -> 0%
where the time goes in v2:
time: 243 us
  Pallas kernels  113 us (47%)
  blocking collectives  80.9 us (33%)
  matrix products  35.1 us (14%)
  local copies, waits for them, and re-layouts  5.68 us (2%)
  starting transfers between devices  4.55 us (2%)
  other arithmetic  2.96 us (1%)
    all_gather x1, blocking collectives, per_device(): lax.all_gather(dense.reshape(steps * row_own, expert_count), ('ep', 'tp')...  80.9 us
    pallas_call x2, Pallas kernels, gather(): pl.pallas_call(functools.partial(gather_kernel, chips, depth), out_shape=...  64.7 us
    pallas_call x1, Pallas kernels, scatter(): pl.pallas_call(functools.partial(scatter_kernel, chips, depth), out_shape...  48.3 us
    dot_general x1, matrix products, per_device(): jnp.dot(hidden, expert_down[0], preferred_element_type=jnp.float32)  9.84 us
    dot_general x1, matrix products, per_device(): jnp.dot(flat_rows, expert_gate[0], preferred_element_type=jnp.float32)  9.12 us
    dot_general x1, matrix products, per_device(): jnp.dot(flat_rows, expert_up[0], preferred_element_type=jnp.float32)  8 us
  transfers between devices with their start and end apart: 1, of which 0 were waited for; matrix products, arithmetic and copies ran while one was open for 0% of the time, Pallas kernels for 0%

profile of v2, /device:TPU:0, one launch (start us, length us, event | category | flops | bytes accessed | tf_op | source)
XLA Modules:
  0.0 242.6 jit_solution(14997242059898510339)
XLA Ops:
  0.0 1.2 copy.37
  1.3 0.9 copy.39
  2.2 0.7 iota_compare_fusion.1
  2.9 0.3 fusion.30
  3.3 2.1 fusion.29
  5.5 0.5 fusion.17
  6.0 0.8 fusion.12
  6.9 0.3 fusion.10
  7.3 1.0 copy.33
  8.4 25.4 %shard_map.118 = bf16[4,2,1,96,2048]{4,3,2,1,0:T(8,128)(2,1)} custom-call(bf16[96,2048]{1,0:T(8,128)(2,1)} %bitcast.74), custom_call_target="tpu_custom_call" | custom-call | tf_op jit(solution)/shard_map/pallas_call | solution.py:96
  33.8 4.6 %convolution_convert_fusion.1 = bf16[768,512]{1,0:T(8,128)(2,1)} fusion(bf16[768,2048]{1,0:T(8,128)(2,1)} %bitcast.72, bf16[2048,512]{1,0:T(8,128)(2,1)S(1)} %copy-done), kind=kOutput, calls=%fused_computation.8 | convolution fusion | flops 1611005952 | bytes 6029312 | tf_op jit(solution)/shard_map/dot_general | solution.py:338
  38.4 4.5 %all-to-all-start = ((bf16[32,24,512]{2,1,0:T(8,128)(2,1)}), bf16[32,24,512]{2,1,0:T(8,128)(2,1)S(1)}, u32[]{:S(2)}, u32[]{:S(2)}) async-start(bf16[32,24,512]{2,1,0:T(8,128)(2,1)} %bitcast.79), calls=%async_computation | async-start | bytes 1572864 | tf_op jit(solution)/shard_map/all_to_all | solution.py:340
  43.0 0.3 fusion.27
  43.4 80.9 %all_gather.3 = f32[768,32]{1,0:T(8,128)S(1)} all-gather(f32[24,32]{1,0:T(8,128)S(1)} %bitcast.84), channel_id=1, replica_groups=mesh['ep'=8,'tp'=4] {'ep','tp'}, dimensions={0}, use_global_device_ids=true | all-gather | bytes 101376 | tf_op jit(solution)/shard_map/all_gather | solution.py:331
  124.3 0.3 dynamic-slice_reduce_fusion
  124.8 0.2 copy.34
  125.2 0.2 fusion.20
  125.5 0.9 multiply_convert_fusion.2
  126.3 39.3 %shard_map.119 = bf16[4,2,4,24,4096]{4,3,2,1,0:T(8,128)(2,1)} custom-call(bf16[24,4096]{1,0:T(8,128)(2,1)} %get-tuple-element.5.x_ref), custom_call_target="tpu_custom_call" | custom-call | tf_op jit(solution)/shard_map/pallas_call | solution.py:96
  165.7 9.1 %fusion.3 = f32[768,768]{1,0:T(8,128)S(1)} fusion(bf16[768,4096]{1,0:T(8,128)(2,1)} %bitcast.69, bf16[1,4096,768]{2,1,0:T(8,128)(2,1)} %param.21), kind=kOutput, calls=%fused_computation.5 | convolution fusion | flops 4831838208 | bytes 14942208 | tf_op jit(solution)/shard_map/dot_general | solution.py:350
  174.8 8.0 %multiply_convert_fusion.1 = bf16[768,768]{1,0:T(8,128)(2,1)S(1)} fusion(f32[768,768]{1,0:T(8,128)S(1)} %fusion.3, bf16[768,4096]{1,0:T(8,128)(2,1)S(1)} %bitcast.70, bf16[1,4096,768]{2,1,0:T(8,128)(2,1)} %param.22), kind=kOutput, calls=%fused_computation.7 | convolution fusion | flops 4835377152 | bytes 16121856 | tf_op jit(solution)/shard_map/dot_general | solution.py:351
  182.8 9.8 %multiply_convert_fusion = bf16[768,4096]{1,0:T(8,128)(2,1)} fusion(f32[768]{0:T(1024)S(1)} %dynamic-slice_reduce_fusion, bf16[768,768]{1,0:T(8,128)(2,1)S(1)} %multiply_convert_fusion.1, bf16[1,768,4096]{2,1,0:T(8,128)(2,1)} %param.23), kind=kOutput, calls=%fused_computation | convolution fusion | flops 4844421120 | bytes 13765632 | tf_op jit(solution)/shard_map/dot_general | solution.py:353
  192.6 48.3 %shard_map.120 = bf16[24,4096]{1,0:T(8,128)(2,1)} custom-call(bf16[4,2,4,24,4096]{4,3,2,1,0:T(8,128)(2,1)} %bitcast.71, f32[24,4096]{1,0:T(8,128)} %get-tuple-element.6.residual_ref), custom_call_target="tpu_custom_call" | custom-call | tf_op jit(solution)/shard_map/pallas_call | solution.py:237
  241.0 1.6 copy.41
  (30 shorter events, 0.8 us)
Async XLA Ops:
  0.0 33.8 %copy-start = (bf16[2048,512]{1,0:T(8,128)(2,1)S(1)}, bf16[2048,512]{1,0:T(8,128)(2,1)}, u32[]{:S(2)}) copy-start(bf16[2048,512]{1,0:T(8,128)(2,1)} %param.18) | copy-start | bytes 6291460
  0.0 6.0 %copy-start.3 = (bf16[2,32,128,128]{3,2,1,0:T(8,128)(2,1)S(1)}, bf16[2,32,128,128]{3,2,1,0:T(8,128)(2,1)}, u32[]{:S(2)}) copy-start(bf16[2,32,128,128]{3,2,1,0:T(8,128)(2,1)} %param.14) | copy-start | bytes 6291460
  33.8 9.2 %copy-start.6 = (f32[3,8,8]{2,1,0:T(8,128)S(1)}, f32[3,8,8]{2,1,0:T(8,128)}, u32[]{:S(2)}) copy-start(f32[3,8,8]{2,1,0:T(8,128)} %param.20) | copy-start | bytes 2308
  33.8 9.4 %copy-start.5 = (s32[3,8,8]{2,1,0:T(8,128)S(1)}, s32[3,8,8]{2,1,0:T(8,128)}, u32[]{:S(2)}) copy-start(s32[3,8,8]{2,1,0:T(8,128)} %param.19) | copy-start | bytes 2308
  38.4 86.8 %copy-start.2 = (bf16[3,8,4096]{2,1,0:T(8,128)(2,1)S(1)}, bf16[3,8,4096]{2,1,0:T(8,128)(2,1)}, u32[]{:S(2)}) copy-start(bf16[3,8,4096]{2,1,0:T(8,128)(2,1)} %param.16) | copy-start | bytes 589828
  38.4 86.2 %all-to-all-start = ((bf16[32,24,512]{2,1,0:T(8,128)(2,1)}), bf16[32,24,512]{2,1,0:T(8,128)(2,1)S(1)}, u32[]{:S(2)}, u32[]{:S(2)}) async-start(bf16[32,24,512]{2,1,0:T(8,128)(2,1)} %bitcast.79), calls=%async_computation | async-start | bytes 1572864 | tf_op jit(solution)/shard_map/all_to_all | solution.py:340
  43.0 82.5 %copy-start.4 = (f32[4096]{0:T(1024)S(1)}, f32[4096]{0:T(1024)}, u32[]{:S(2)}) copy-start(f32[4096]{0:T(1024)} %param.17) | copy-start | bytes 49156
  165.7 9.1 %copy-start.1 = (bf16[4,2,4,24,4096]{4,3,2,1,0:T(8,128)(2,1)S(1)}, bf16[4,2,4,24,4096]{4,3,2,1,0:T(8,128)(2,1)}, u32[]{:S(2)}) copy-start(bf16[4,2,4,24,4096]{4,3,2,1,0:T(8,128)(2,1)} %shard_map.119) | copy-start | bytes 18874372

commit v3 on v2

--- a/solution.py
+++ b/solution.py
@@ -322,23 +322,25 @@
     width = hidden_in.shape[2]
     cols = w_out.shape[1]
     expert_count = ep_count * tp_count * expert_gate.shape[0]
-    mine = lax.axis_index("ep") * tp_count + lax.axis_index("tp")
 
     weights = gate_scores / jnp.sum(gate_scores, axis=-1, keepdims=True)
     named = routes[..., None] == jnp.arange(expert_count, dtype=jnp.int32)
     dense = jnp.sum(jnp.where(named, weights[..., None], 0.0), axis=2)
 
-    all_dense = lax.all_gather(
-        dense.reshape(steps * row_own, expert_count), ("ep", "tp"), axis=0, tiled=True
-    )
-    my_weight = lax.dynamic_slice_in_dim(all_dense, mine, 1, axis=1)
+    by_expert = dense.reshape(steps * row_own, expert_count).T[..., None]
+    high = lax.reduce_precision(by_expert, 8, 7)
+    middle = lax.reduce_precision(by_expert - high, 8, 7)
+    pieces = jnp.concatenate([high, middle, by_expert - high - middle], axis=2)
+    pieces = jnp.pad(pieces, ((0, 0), (0, 0), (0, 125))).astype(jnp.bfloat16)
 
     attended = attend(query, step_key_value, key_value_cache, lengths, tp_count)
     everyone = gather(attended, chips, 1, 1)
     partial_sums = jnp.dot(everyone, w_out, preferred_element_type=jnp.float32)
     partial_sums = partial_sums.astype(jnp.bfloat16).reshape(-1, steps * row_own, cols)
-    arrived = lax.all_to_all(partial_sums, ("ep", "tp"), split_axis=0, concat_axis=0, tiled=True)
-    arrived = arrived.reshape(ep_count, tp_count, steps * row_own, cols)
+    outgoing = jnp.concatenate([partial_sums, pieces], axis=2)
+    arrived = lax.all_to_all(outgoing, ("ep", "tp"), split_axis=0, concat_axis=0, tiled=True)
+    my_weight = jnp.sum(arrived[..., cols : cols + 3].astype(jnp.float32), axis=2).reshape(-1, 1)
+    arrived = arrived[..., :cols].reshape(ep_count, tp_count, steps * row_own, cols)
     projected = jnp.sum(arrived.astype(jnp.float32), axis=1).astype(jnp.bfloat16)
     row_major = projected.transpose(1, 0, 2).reshape(steps * row_own, width)
     own = hidden_in.reshape(steps * row_own, width)

time: 243 us -> 188 us (0.77)
  blocking collectives: 80.9 us -> 28.1 us
  starting transfers between devices: 4.55 us -> 0 us
  Pallas kernels: 113 us -> 116 us
    all_gather x1 -> x0, blocking collectives: 80.9 us -> none  [per_device(): lax.all_gather(dense.reshape(steps * row_own, expert_count), ('ep', 'tp')...]
    all_to_all x0 -> x1, blocking collectives: none -> 28.1 us  [per_device(): lax.all_to_all(outgoing, ('ep', 'tp'), split_axis=0, concat_axis=0, tiled...]
    all_to_all x1 -> x0, starting transfers between devices: 4.55 us -> none  [per_device(): lax.all_to_all(partial_sums, ('ep', 'tp'), split_axis=0, concat_axis=0, t...]
    pallas_call x2, Pallas kernels: 64.7 us -> 67.3 us  [gather(): pl.pallas_call(functools.partial(gather_kernel, chips, depth), out_shape=...]
  transfers between devices with their start and end apart: 1 -> 0, of which waited for: 0 -> 0; matrix products, arithmetic and copies ran while one was open for 0% -> 0% of each run, Pallas kernels for 0% -> 0%
where the time goes in v3:
time: 188 us
  Pallas kernels  116 us (62%)
  matrix products  33 us (18%)
  blocking collectives  28.1 us (15%)
  local copies, waits for them, and re-layouts  5.82 us (3%)
  other arithmetic  4.66 us (2%)
    pallas_call x2, Pallas kernels, gather(): pl.pallas_call(functools.partial(gather_kernel, chips, depth), out_shape=...  67.3 us
    pallas_call x1, Pallas kernels, scatter(): pl.pallas_call(functools.partial(scatter_kernel, chips, depth), out_shape...  48.5 us
    all_to_all x1, blocking collectives, per_device(): lax.all_to_all(outgoing, ('ep', 'tp'), split_axis=0, concat_axis=0, tiled...  28.1 us
    dot_general x1, matrix products, per_device(): jnp.dot(hidden, expert_down[0], preferred_element_type=jnp.float32)  9.85 us
    dot_general x1, matrix products, per_device(): jnp.dot(flat_rows, expert_gate[0], preferred_element_type=jnp.float32)  9.1 us
    dot_general x1, matrix products, per_device(): jnp.dot(flat_rows, expert_up[0], preferred_element_type=jnp.float32)  8 us
    unnamed x14, local copies, waits for them, and re-layouts  4.12 us

profile of v3, /device:TPU:0, one launch (start us, length us, event | category | flops | bytes accessed | tf_op | source)
XLA Modules:
  0.0 187.6 jit_solution(1164109557993484563)
XLA Ops:
  0.0 0.9 iota_compare_fusion.2
  0.9 0.9 fusion.33
  1.8 0.8 select_reduce_fusion
  2.6 0.8 copy.43
  3.5 0.3 copy.39
  3.8 1.2 copy.41
  5.0 0.3 fusion.36
  5.5 0.9 fusion.35
  6.5 0.5 fusion.19
  7.0 0.8 fusion.13
  7.8 0.3 fusion.11
  8.3 1.0 copy.35
  9.3 25.4 %shard_map.118 = bf16[4,2,1,96,2048]{4,3,2,1,0:T(8,128)(2,1)} custom-call(bf16[96,2048]{1,0:T(8,128)(2,1)} %bitcast.94), custom_call_target="tpu_custom_call" | custom-call | tf_op jit(solution)/shard_map/pallas_call | solution.py:96
  34.8 3.7 %convolution_convert_fusion.1 = bf16[768,512]{1,0:T(8,128)(2,1)S(1)} fusion(bf16[768,2048]{1,0:T(8,128)(2,1)} %bitcast.92, bf16[2048,512]{1,0:T(8,128)(2,1)S(1)} %copy-done), kind=kOutput, calls=%fused_computation.10 | convolution fusion | flops 1611005952 | bytes 6029312 | tf_op jit(solution)/shard_map/dot_general | solution.py:338
  38.5 28.1 %all_to_all.5 = bf16[32,24,640]{2,1,0:T(8,128)(2,1)S(1)} all-to-all(bf16[32,24,640]{2,1,0:T(8,128)(2,1)S(1)} %fusion.18), channel_id=1, replica_groups=mesh['ep'=8,'tp'=4] {'ep','tp'}, dimensions={0} | all-to-all | bytes 1966080 | tf_op jit(solution)/shard_map/all_to_all | solution.py:341
  66.6 0.2 convert_reduce_fusion
  67.1 0.2 copy.37
  67.8 0.9 multiply_convert_fusion.2
  68.6 41.8 %shard_map.119 = bf16[4,2,4,24,4096]{4,3,2,1,0:T(8,128)(2,1)} custom-call(bf16[24,4096]{1,0:T(8,128)(2,1)} %get-tuple-element.5.x_ref), custom_call_target="tpu_custom_call" | custom-call | tf_op jit(solution)/shard_map/pallas_call | solution.py:96
  110.5 9.1 %fusion.3 = f32[768,768]{1,0:T(8,128)S(1)} fusion(bf16[768,4096]{1,0:T(8,128)(2,1)} %bitcast.89, bf16[1,4096,768]{2,1,0:T(8,128)(2,1)} %param.21), kind=kOutput, calls=%fused_computation.5 | convolution fusion | flops 4831838208 | bytes 14942208 | tf_op jit(solution)/shard_map/dot_general | solution.py:352
  119.6 8.0 %multiply_convert_fusion.1 = bf16[768,768]{1,0:T(8,128)(2,1)S(1)} fusion(f32[768,768]{1,0:T(8,128)S(1)} %fusion.3, bf16[768,4096]{1,0:T(8,128)(2,1)S(1)} %bitcast.90, bf16[1,4096,768]{2,1,0:T(8,128)(2,1)} %param.22), kind=kOutput, calls=%fused_computation.7 | convolution fusion | flops 4835377152 | bytes 16121856 | tf_op jit(solution)/shard_map/dot_general | solution.py:353
  127.6 9.8 %multiply_convert_fusion = bf16[768,4096]{1,0:T(8,128)(2,1)} fusion(f32[768]{0:T(1024)S(1)} %mul.60, bf16[768,768]{1,0:T(8,128)(2,1)S(1)} %multiply_convert_fusion.1, bf16[1,768,4096]{2,1,0:T(8,128)(2,1)} %param.23), kind=kOutput, calls=%fused_computation | convolution fusion | flops 4844421120 | bytes 13765632 | tf_op jit(solution)/shard_map/dot_general | solution.py:355
  137.5 48.5 %shard_map.120 = bf16[24,4096]{1,0:T(8,128)(2,1)} custom-call(bf16[4,2,4,24,4096]{4,3,2,1,0:T(8,128)(2,1)} %bitcast.91, f32[24,4096]{1,0:T(8,128)} %get-tuple-element.6.residual_ref), custom_call_target="tpu_custom_call" | custom-call | tf_op jit(solution)/shard_map/pallas_call | solution.py:237
  185.9 1.6 copy.45
  (29 shorter events, 1.1 us)
Async XLA Ops:
  0.0 34.7 %copy-start = (bf16[2048,512]{1,0:T(8,128)(2,1)S(1)}, bf16[2048,512]{1,0:T(8,128)(2,1)}, u32[]{:S(2)}) copy-start(bf16[2048,512]{1,0:T(8,128)(2,1)} %param.18) | copy-start | bytes 6291460
  3.7 1.7 copy-start.3
  66.6 0.9 copy-start.2
  66.8 0.9 copy-start.4
  110.5 9.1 %copy-start.1 = (bf16[4,2,4,24,4096]{4,3,2,1,0:T(8,128)(2,1)S(1)}, bf16[4,2,4,24,4096]{4,3,2,1,0:T(8,128)(2,1)}, u32[]{:S(2)}) copy-start(bf16[4,2,4,24,4096]{4,3,2,1,0:T(8,128)(2,1)} %shard_map.119) | copy-start | bytes 18874372
